TPU v7x, 32 devices: a whole 2x2x4 slice. The times are simulated.
32 devices in a mesh: row: 16 (over z, y, x), col: 2 (over core).
Axes of the slice: x: 2, y: 2, z: 4, core: 2. Of those that a mesh axis runs over, the one named last changes fastest.
Arguments:
- queries: bfloat16 [16384, 1024], P(('row', 'col')), may hold values from -150 to 150
- keys: bfloat16 [16384, 128], P(('col', 'row')), may hold values from -6.1 to 6.1
- values: bfloat16 [16384, 128], P(('col', 'row')), may hold values from -6 to 6
- row_ptr: int32 [129], replicated, may hold values from 0 to 2048, as said below
- col_blocks: int32 [2048], replicated, may hold values from 0 to 127, as said below
- w_out: bfloat16 [1024, 8192], replicated, may hold values from -0.1875 to 0.1875
Outputs:
- projected: bfloat16 [16384, 8192], P(('row', 'col'))
Inputs may be any that keep to these rules, and one draw needn't show every extreme that they name: row_ptr[0] is 0 and row_ptr never falls; block-row b lists row_ptr[b+1] - row_ptr[b] blocks, 1 to 31; row_ptr[g * 8] = g * 8 * 16 for every g; in every group of 8 consecutive block-rows some block-row lists exactly 31 blocks. col_blocks[e] lies in key group e mod 2, that is between (e mod 2) * 64 and (e mod 2) * 64 + 63; the blocks listed for one block-row are distinct.
All inputs are finite; a program needn't handle non-finite values.
Results may differ from a plain program's by a relative error of at most 0.0055.
Values may be sent and summed in bfloat16 or wider, within the bound.
A program may use at most 192 MiB of HBM per device.

v0:
```python
import functools
import math

import jax
import jax.numpy as jnp
from jax import lax
from jax.experimental import pallas as pl
from jax.experimental.pallas import tpu as pltpu
from jax.sharding import PartitionSpec as P

HEAD_DIM = 128
BLOCK = 128
ONES = 16
CHUNK = 256
LOW = -1e30
RATE = HEAD_DIM ** (-0.5) * math.log2(math.e)
MESH = pl.DeviceIdType.MESH
VMEM_LIMIT = 60 * 1024 * 1024


def grid_of(chips):
    side = 1
    while 4 * (2 * side) ** 2 <= chips:
        side *= 2
    return chips // (side * side), side, side


def near(here, k, size):
    if size == 2:
        return 1 - here
    below, above = here, size - 1 - here
    room = jnp.minimum(below, above)
    side = jnp.where(above >= below, 1, -1)
    both = (k + 1) // 2 * (1 if k % 2 else -1)
    return here + side * jnp.where(k <= 2 * room, both, k - room)


def attend_kernel(
    sizes, slots, ptr_ref, cols_ref, q_ref, k_ref, v_ref, out_ref,
    q_other, k_all, vt_all, qt, weights, alphas, stats, scores_a, scores_b, acc, top,
    sent, sent_stat, got, got_stat, xsem, ssem, rsem,
):
    row, col = lax.axis_index("row"), lax.axis_index("col")
    zs, ys, xs = sizes
    here = (row // (ys * xs), row // xs % ys, row % xs)
    shard = k_ref.shape[0] // BLOCK
    part_blocks = shard // 2
    half_rows = q_ref.shape[0] // BLOCK
    width = q_ref.shape[1]
    chunks = [slice(start, start + CHUNK) for start in range(0, width, CHUNK)]
    heads = [slice(start, start + HEAD_DIM) for start in range(0, width, HEAD_DIM)]

    def number(place):
        return (place[0] * ys + place[1]) * xs + place[2]

    def beside(axis, step):
        there = list(here)
        there[axis] = here[axis] + step
        inside = jnp.logical_and(there[axis] >= 0, there[axis] < sizes[axis])
        return number(there), inside

    for block in range(shard):
        rows = slice(block * BLOCK, (block + 1) * BLOCK)
        k_all[row * shard + block] = k_ref[rows, :]
        vt_all[row * shard + block] = v_ref[rows, :].T

    barrier = pltpu.get_barrier_semaphore()
    greeted = 1
    for axis in range(3):
        for step in (-1, 1):
            there, inside = beside(axis, step)

            @pl.when(inside)
            def _():
                pl.semaphore_signal(barrier, inc=1, device_id=(there, col), device_id_type=MESH)

            greeted = greeted + jnp.where(inside, 1, 0)
    pl.semaphore_signal(barrier, inc=1, device_id=(row, 1 - col), device_id_type=MESH)
    pl.semaphore_wait(barrier, greeted)

    orders = ((0, 2, 1), (0, 1, 2)) * 2
    key_pieces, value_pieces = (0, 1), (2, 3)
    sends = []

    def copy(piece, origin, slot, there):
        held = (k_all if piece < 2 else vt_all).at[
            pl.ds(origin * shard + piece % 2 * part_blocks, part_blocks)
        ]
        return pltpu.make_async_remote_copy(
            src_ref=held,
            dst_ref=held,
            send_sem=ssem.at[piece, origin, slot],
            recv_sem=rsem.at[piece, origin],
            device_id=(there, col),
            device_id_type=MESH,
        )

    def send(piece, origin, axis, step, wanted=None):
        there, inside = beside(axis, step)
        if wanted is not None:
            inside = jnp.logical_and(inside, wanted)
        slot = axis * 2 + (step + 1) // 2

        @pl.when(inside)
        def _():
            copy(piece, origin, slot, there).start()

        sends.append((inside, piece, origin, slot, there))

    def placed(piece, ks):
        place = list(here)
        for axis, k in zip(orders[piece], ks):
            if k:
                place[axis] = near(here[axis], k, sizes[axis])
        return place

    def arrive(piece, level, ks):
        place = placed(piece, ks)
        origin = number(place)
        copy(piece, origin, 0, row).wait_recv()
        order = orders[piece]
        axis = order[level]
        if sizes[axis] > 2:
            send(piece, origin, axis, 1, place[axis] < here[axis])
            send(piece, origin, axis, -1, place[axis] > here[axis])
        for later in order[level + 1 :]:
            for step in (-1, 1):
                send(piece, origin, later, step)

    def lines(pieces, k):
        for piece in pieces:
            arrive(piece, 0, (k, 0, 0))

    def planes(pieces, k):
        for piece in pieces:
            for k2 in range(1, sizes[orders[piece][1]]):
                arrive(piece, 1, (k, k2, 0))

    def ends(pieces):
        for k in range(zs):
            for piece in pieces:
                for k2 in range(sizes[orders[piece][1]]):
                    for k3 in range(1, sizes[orders[piece][2]]):
                        arrive(piece, 2, (k, k2, k3))

    def swap(source, target, index):
        return pltpu.make_async_remote_copy(
            src_ref=source,
            dst_ref=target,
            send_sem=xsem.at[2 * index],
            recv_sem=xsem.at[2 * index + 1],
            device_id=(row, 1 - col),
            device_id_type=MESH,
        )

    for piece in key_pieces:
        for axis in orders[piece]:
            for step in (-1, 1):
                send(piece, row, axis, step)
    to_other = swap(q_ref, q_other, 0)
    to_other.start()

    def turn(ref, begin):
        for i in range(half_rows):
            for head in heads:
                qt[begin + i, :, head] = ref[i * BLOCK : (i + 1) * BLOCK, head].T

    turn(q_ref, half_rows)
    acc[...] = jnp.zeros_like(acc)
    top[...] = jnp.full_like(top, LOW)

    planes(key_pieces, 0)
    for k in range(1, zs):
        lines(key_pieces, k)
        if k < zs - 1:
            planes(key_pieces, k)
    for piece in value_pieces:
        for step in (-1, 1):
            send(piece, row, 0, step)
    if zs > 1:
        planes(key_pieces, zs - 1)
    for piece in value_pieces:
        for axis in orders[piece][1:]:
            for step in (-1, 1):
                send(piece, row, axis, step)
    to_other.wait()
    turn(q_other, 0)

    base = col * k_all.shape[0]
    firsts, counts, starts, pairs = [], [], [], []
    listed = 0
    for i in range(2 * half_rows):
        half = 1 - col if i < half_rows else col
        block_row = (row * 2 + half) * half_rows + i % half_rows
        begin, end = ptr_ref[block_row], ptr_ref[block_row + 1]
        first = begin + ((begin + col) & 1)
        count = jnp.maximum(end - first + 1, 0) >> 1
        firsts.append(first)
        counts.append(count)
        pairs.append((count + 1) >> 1)
        starts.append(listed)
        listed = listed + pairs[-1]

    def block_at(entry):
        block = cols_ref[jnp.clip(entry, 0, cols_ref.shape[0] - 1)] - base
        return jnp.clip(block, 0, k_all.shape[0] - 1)

    def slot_of(p):
        live = p < listed
        at = jnp.clip(p, 0, jnp.maximum(listed - 1, 0))
        i, first, count, start = 0, firsts[0], counts[0], starts[0]
        for j in range(1, 2 * half_rows):
            reached = at >= starts[j]
            i = jnp.where(reached, j, i)
            first = jnp.where(reached, firsts[j], first)
            count = jnp.where(reached, counts[j], count)
            start = jnp.where(reached, starts[j], start)
        t = at - start
        both = 2 * t + 1 < count
        entry = first + 4 * t
        a = block_at(entry)
        b = block_at(jnp.where(both, entry + 2, entry))
        live_a = jnp.where(live, 1.0, 0.0)
        live_b = jnp.where(jnp.logical_and(live, both), 1.0, 0.0)
        opened = jnp.where(jnp.logical_and(live, t == 0), 1, 0)
        return i, a, b, live_a, live_b, opened

    def score(slot, part, into):
        i, a, b = slot[:3]
        keys = jnp.concatenate([k_all[a], k_all[b]], axis=0)
        into[:, part] = jnp.dot(keys, qt[i, :, part], preferred_element_type=jnp.float32)

    def soften(p, scores_now, scores_next):
        following = slot_of(p + 1)
        fresh = jnp.full((1, CHUNK), slot_of(p)[5], jnp.int32) == 1
        for part in chunks:
            score(following, part, scores_next)
            scores = scores_now[:, part]
            old = jnp.where(fresh, LOW, top[:, part])
            new = jnp.maximum(old, jnp.max(scores, axis=0, keepdims=True))
            weights[p, :, part] = jnp.exp2((scores - new) * RATE).astype(weights.dtype)
            alphas[p, :, part] = jnp.exp2((old - new) * RATE)
            stats[p, 0:1, part] = new
            top[:, part] = new

    lines(value_pieces, 1) if zs > 1 else None
    ends(key_pieces)
    opening = slot_of(0)
    for part in chunks:
        score(opening, part, scores_a)

    duties = [functools.partial(planes, value_pieces, 0)]
    for k in range(2, zs):
        duties.append(functools.partial(lines, value_pieces, k))
        duties.append(functools.partial(planes, value_pieces, k - 1))
    if zs > 1:
        duties.append(functools.partial(planes, value_pieces, zs - 1))

    for index, duty in enumerate(duties):
        begin = min(2 * index, slots // 2)
        end = min(begin + 2, slots // 2) if index < len(duties) - 1 else slots // 2
        duty()

        def two(t, carry):
            soften(2 * t, scores_a, scores_b)
            soften(2 * t + 1, scores_b, scores_a)
            return carry

        lax.fori_loop(begin, end, two, 0)

    ends(value_pieces)

    def add(p, carry):
        _, a, b, live_a, live_b, _ = slot_of(p)

        def one(block, live):
            ones = jnp.ones((ONES, BLOCK), vt_all.dtype)
            whole = jnp.concatenate([vt_all[block], ones], axis=0)
            return whole * jnp.full(whole.shape, live, jnp.float32).astype(whole.dtype)

        values = jnp.concatenate([one(a, live_a), one(b, live_b)], axis=1)
        for part in chunks:
            term = jnp.dot(values, weights[p, :, part], preferred_element_type=jnp.float32)
            total = acc[:, part] * alphas[p, :, part] + term
            acc[:, part] = total
            weights[p, :HEAD_DIM, part] = total[:HEAD_DIM].astype(weights.dtype)
            stats[p, 1:2, part] = total[HEAD_DIM : HEAD_DIM + 1]
        return carry

    lax.fori_loop(0, slots, add, 0)

    def row_state(i):
        some = jnp.full((1, width), pairs[i], jnp.int32) > 0
        at = jnp.clip(starts[i] + pairs[i] - 1, 0, slots - 1)
        peak = jnp.where(some, stats[at, 0:1, :], LOW)
        total = jnp.where(some, stats[at, 1:2, :], 0.0)
        return peak, total, weights[at, :HEAD_DIM, :]

    for i in range(half_rows):
        peak, total, summed = row_state(i)
        sent[i] = summed
        sent_stat[i] = jnp.concatenate(
            [peak, total, jnp.zeros((6, width), jnp.float32)], axis=0
        )
    swaps = [swap(sent, got, 1), swap(sent_stat, got_stat, 2)]
    for moving in swaps:
        moving.start()
    for inside, piece, origin, slot, there in sends:

        @pl.when(inside)
        def _():
            copy(piece, origin, slot, there).wait_send()

    for moving in swaps:
        moving.wait()
    for i in range(half_rows):
        max_a, sum_a, out_a = row_state(half_rows + i)
        max_b, sum_b = got_stat[i, 0:1, :], got_stat[i, 1:2, :]
        peak = jnp.maximum(max_a, max_b)
        scale_a = jnp.where(sum_a > 0.0, jnp.exp2((max_a - peak) * RATE), 0.0)
        scale_b = jnp.where(sum_b > 0.0, jnp.exp2((max_b - peak) * RATE), 0.0)
        total = sum_a * scale_a + sum_b * scale_b
        scale_a, scale_b = scale_a / total, scale_b / total
        for head in heads:
            joined = (
                out_a[:, head].astype(jnp.float32) * scale_a[:, head]
                + got[i, :, head].astype(jnp.float32) * scale_b[:, head]
            )
            out_ref[i * BLOCK : (i + 1) * BLOCK, head] = joined.T.astype(out_ref.dtype)


def attend(sizes, entries, row_ptr, col_blocks, queries, keys, values):
    chips = sizes[0] * sizes[1] * sizes[2]
    rows, width = queries.shape[0] // BLOCK, queries.shape[1]
    slots = (entries + 2 * rows) // 2
    slots += slots % 2
    blocks = chips * keys.shape[0] // BLOCK
    in_vmem = pl.BlockSpec(memory_space=pltpu.VMEM)
    in_smem = pl.BlockSpec(memory_space=pltpu.SMEM)
    bf16, f32 = jnp.bfloat16, jnp.float32
    return pl.pallas_call(
        functools.partial(attend_kernel, sizes, slots),
        out_shape=jax.ShapeDtypeStruct(queries.shape, queries.dtype),
        in_specs=[in_smem] * 2 + [in_vmem] * 3,
        out_specs=in_vmem,
        scratch_shapes=[
            pltpu.VMEM(queries.shape, bf16),
            pltpu.VMEM((blocks, BLOCK, HEAD_DIM), bf16),
            pltpu.VMEM((blocks, HEAD_DIM, BLOCK), bf16),
            pltpu.VMEM((2 * rows, HEAD_DIM, width), bf16),
            pltpu.VMEM((slots, 2 * BLOCK, width), bf16),
            pltpu.VMEM((slots, 1, width), f32),
            pltpu.VMEM((slots, 8, width), f32),
            pltpu.VMEM((2 * BLOCK, width), f32),
            pltpu.VMEM((2 * BLOCK, width), f32),
            pltpu.VMEM((HEAD_DIM + ONES, width), f32),
            pltpu.VMEM((1, width), f32),
            pltpu.VMEM((rows, HEAD_DIM, width), bf16),
            pltpu.VMEM((rows, 8, width), f32),
            pltpu.VMEM((rows, HEAD_DIM, width), bf16),
            pltpu.VMEM((rows, 8, width), f32),
            pltpu.SemaphoreType.DMA((6,)),
            pltpu.SemaphoreType.DMA((4, chips, 6)),
            pltpu.SemaphoreType.DMA((4, chips)),
        ],
        compiler_params=pltpu.CompilerParams(
            collective_id=0, has_side_effects=True, vmem_limit_bytes=VMEM_LIMIT
        ),
        name="attend",
    )(row_ptr, col_blocks, queries, keys, values)


def project_kernel(attention, w_ref, o_ref):
    o_ref[...] = jnp.dot(
        attention[...], w_ref[...], preferred_element_type=jnp.float32
    ).astype(o_ref.dtype)


def project(attention, w_out):
    tokens, width = attention.shape
    columns = w_out.shape[1]
    tile = 1024
    return pl.pallas_call(
        project_kernel,
        out_shape=jax.ShapeDtypeStruct((tokens, columns), jnp.bfloat16),
        grid=(columns // tile,),
        in_specs=[
            pl.BlockSpec((tokens, width), lambda j: (0, 0)),
            pl.BlockSpec((width, tile), lambda j: (0, j)),
        ],
        out_specs=pl.BlockSpec((tokens, tile), lambda j: (0, j)),
        compiler_params=pltpu.CompilerParams(vmem_limit_bytes=VMEM_LIMIT),
        cost_estimate=pl.CostEstimate(
            flops=2 * tokens * width * columns,
            bytes_accessed=2 * (width * columns + tokens * columns),
            transcendentals=0,
        ),
        name="project",
    )(attention, w_out)


def local(queries, keys, values, row_ptr, col_blocks, w_out):
    chips = lax.axis_size("row")
    entries = col_blocks.shape[0] // (chips * lax.axis_size("col"))
    attention = attend(
        grid_of(chips), entries, row_ptr, col_blocks, queries, keys, values
    )
    return project(attention, w_out)


def solution(mesh):
    in_specs = (
        P(("row", "col"), None),
        P(("col", "row"), None),
        P(("col", "row"), None),
        P(),
        P(),
        P(),
    )
    out_specs = P(("row", "col"), None)
    return jax.shard_map(local, mesh=mesh, in_specs=in_specs, out_specs=out_specs, check_vma=False)
```

profile of v0, /device:TPU:0, one launch (start us, length us, event | category | flops | bytes accessed | tf_op | source)
XLA Modules:
  0.0 81.9 jit_solution(16351583562703476592)
XLA Ops:
  0.0 66.4 %attend.1.attention = bf16[512,1024]{1,0:T(8,128)(2,1)} custom-call(s32[129]{0:T(256)} %ptr_ref.1, s32[2048]{0:T(1024)} %cols_ref.1, bf16[512,1024]{1,0:T(8,128)(2,1)} %q_ref.1, bf16[512,128]{1,0:T(8,128)(2,1)} %k_ref.1, bf16[512,128]{1,0:T(8,128)(2,1)} %v_ref.1), custom_call_target="tpu_custom_call" | custom-call | tf_op jit(solution)/shard_map/attend/pallas_call | solution.py:341
  66.4 15.5 %project.1 = bf16[512,8192]{1,0:T(8,128)(2,1)} custom-call(bf16[512,1024]{1,0:T(8,128)(2,1)} %attend.1.attention, bf16[1024,8192]{1,0:T(8,128)(2,1)} %w_ref.1), custom_call_target="tpu_custom_call" | custom-call | flops 8589934592 | bytes 25165824 | tf_op jit(solution)/shard_map/project/pallas_call | solution.py:383
where the time goes:
time: 82.3 us; the launch traced here: 81.9 us
  Pallas kernels  81.9 us (100%)
    pallas_call x1, Pallas kernels, attend(): pl.pallas_call(functools.partial(attend_kernel, sizes, slots), out_shape=...  66.4 us
    pallas_call x1, Pallas kernels, project(): pl.pallas_call(project_kernel, out_shape=jax.ShapeDtypeStruct((tokens, co...  15.5 us

commit v1 on v0

--- a/solution.py
+++ b/solution.py
@@ -16,6 +16,7 @@
 RATE = HEAD_DIM ** (-0.5) * math.log2(math.e)
 MESH = pl.DeviceIdType.MESH
 VMEM_LIMIT = 60 * 1024 * 1024
+SLOW = 30
 
 
 def grid_of(chips):
@@ -177,12 +178,12 @@
     for piece in value_pieces:
         for step in (-1, 1):
             send(piece, row, 0, step)
-    if zs > 1:
-        planes(key_pieces, zs - 1)
     for piece in value_pieces:
         for axis in orders[piece][1:]:
             for step in (-1, 1):
                 send(piece, row, axis, step)
+    if zs > 1:
+        planes(key_pieces, zs - 1)
     to_other.wait()
     turn(q_other, 0)
 
@@ -243,22 +244,23 @@
             stats[p, 0:1, part] = new
             top[:, part] = new
 
-    lines(value_pieces, 1) if zs > 1 else None
+    if zs > 1:
+        lines(value_pieces, 1)
+    planes(value_pieces, 0)
     ends(key_pieces)
     opening = slot_of(0)
     for part in chunks:
         score(opening, part, scores_a)
 
-    duties = [functools.partial(planes, value_pieces, 0)]
+    duties = []
     for k in range(2, zs):
-        duties.append(functools.partial(lines, value_pieces, k))
-        duties.append(functools.partial(planes, value_pieces, k - 1))
+        duties.append((3 * (k - 2), functools.partial(lines, value_pieces, k)))
+        duties.append((3 * (k - 2) + 1, functools.partial(planes, value_pieces, k - 1)))
     if zs > 1:
-        duties.append(functools.partial(planes, value_pieces, zs - 1))
-
-    for index, duty in enumerate(duties):
-        begin = min(2 * index, slots // 2)
-        end = min(begin + 2, slots // 2) if index < len(duties) - 1 else slots // 2
+        duties.append((3 * (zs - 2), functools.partial(planes, value_pieces, zs - 1)))
+    turns = [min(turn, slots // 2) for turn, _ in duties] + [slots // 2]
+
+    for (_, duty), begin, end in zip(duties, turns, turns[1:]):
         duty()
 
         def two(t, carry):
@@ -338,33 +340,41 @@
     in_vmem = pl.BlockSpec(memory_space=pltpu.VMEM)
     in_smem = pl.BlockSpec(memory_space=pltpu.SMEM)
     bf16, f32 = jnp.bfloat16, jnp.float32
+    buffers = [
+        (queries.shape, bf16),
+        ((blocks, BLOCK, HEAD_DIM), bf16),
+        ((blocks, HEAD_DIM, BLOCK), bf16),
+        ((2 * rows, HEAD_DIM, width), bf16),
+        ((slots, 2 * BLOCK, width), bf16),
+        ((slots, 1, width), f32),
+        ((slots, 8, width), f32),
+        ((2 * BLOCK, width), f32),
+        ((2 * BLOCK, width), f32),
+        ((HEAD_DIM + ONES, width), f32),
+        ((1, width), f32),
+        ((rows, HEAD_DIM, width), bf16),
+        ((rows, 8, width), f32),
+        ((rows, HEAD_DIM, width), bf16),
+        ((rows, 8, width), f32),
+    ]
     return pl.pallas_call(
         functools.partial(attend_kernel, sizes, slots),
         out_shape=jax.ShapeDtypeStruct(queries.shape, queries.dtype),
         in_specs=[in_smem] * 2 + [in_vmem] * 3,
         out_specs=in_vmem,
-        scratch_shapes=[
-            pltpu.VMEM(queries.shape, bf16),
-            pltpu.VMEM((blocks, BLOCK, HEAD_DIM), bf16),
-            pltpu.VMEM((blocks, HEAD_DIM, BLOCK), bf16),
-            pltpu.VMEM((2 * rows, HEAD_DIM, width), bf16),
-            pltpu.VMEM((slots, 2 * BLOCK, width), bf16),
-            pltpu.VMEM((slots, 1, width), f32),
-            pltpu.VMEM((slots, 8, width), f32),
-            pltpu.VMEM((2 * BLOCK, width), f32),
-            pltpu.VMEM((2 * BLOCK, width), f32),
-            pltpu.VMEM((HEAD_DIM + ONES, width), f32),
-            pltpu.VMEM((1, width), f32),
-            pltpu.VMEM((rows, HEAD_DIM, width), bf16),
-            pltpu.VMEM((rows, 8, width), f32),
-            pltpu.VMEM((rows, HEAD_DIM, width), bf16),
-            pltpu.VMEM((rows, 8, width), f32),
+        scratch_shapes=[pltpu.VMEM(shape, kind) for shape, kind in buffers]
+        + [
             pltpu.SemaphoreType.DMA((6,)),
             pltpu.SemaphoreType.DMA((4, chips, 6)),
             pltpu.SemaphoreType.DMA((4, chips)),
         ],
         compiler_params=pltpu.CompilerParams(
             collective_id=0, has_side_effects=True, vmem_limit_bytes=VMEM_LIMIT
+        ),
+        cost_estimate=pl.CostEstimate(
+            flops=entries * 4 * BLOCK * width * HEAD_DIM,
+            bytes_accessed=SLOW * 4 * blocks * BLOCK * HEAD_DIM,
+            transcendentals=entries * BLOCK * width,
         ),
         name="attend",
     )(row_ptr, col_blocks, queries, keys, values)

time: 82.3 us -> 83.4 us (1.013)
  Pallas kernels: 81.9 us -> 83 us
    pallas_call x1, Pallas kernels: 66.4 us -> 67.5 us  [attend(): pl.pallas_call(functools.partial(attend_kernel, sizes, slots), out_shape=...]
where the time goes in v1:
time: 83.4 us; the launch traced here: 83 us
  Pallas kernels  83 us (100%)
    pallas_call x1, Pallas kernels, attend(): pl.pallas_call(functools.partial(attend_kernel, sizes, slots), out_shape=...  67.5 us
    pallas_call x1, Pallas kernels, project(): pl.pallas_call(project_kernel, out_shape=jax.ShapeDtypeStruct((tokens, co...  15.5 us

profile of v1, /device:TPU:0, one launch (start us, length us, event | category | flops | bytes accessed | tf_op | source)
XLA Modules:
  0.0 83.0 jit_solution(16097014513171551968)
XLA Ops:
  0.0 67.5 %attend.1.attention = bf16[512,1024]{1,0:T(8,128)(2,1)} custom-call(s32[129]{0:T(256)} %ptr_ref.1, s32[2048]{0:T(1024)} %cols_ref.1, bf16[512,1024]{1,0:T(8,128)(2,1)} %q_ref.1, bf16[512,128]{1,0:T(8,128)(2,1)} %k_ref.1, bf16[512,128]{1,0:T(8,128)(2,1)} %v_ref.1), custom_call_target="tpu_custom_call" | custom-call | flops 4294967296 | bytes 125829120 | tf_op jit(solution)/shard_map/attend/pallas_call | solution.py:360
  67.5 15.5 %project.1 = bf16[512,8192]{1,0:T(8,128)(2,1)} custom-call(bf16[512,1024]{1,0:T(8,128)(2,1)} %attend.1.attention, bf16[1024,8192]{1,0:T(8,128)(2,1)} %w_ref.1), custom_call_target="tpu_custom_call" | custom-call | flops 8589934592 | bytes 25165824 | tf_op jit(solution)/shard_map/project/pallas_call | solution.py:393
